TPU v7x, 32 devices: a whole 2x2x4 slice. The times are simulated.
32 devices in a mesh: design: 2 (over x), gx: 4 (over y, core), gy: 4 (over z).
Axes of the slice: x: 2, y: 2, z: 4, core: 2. Of those that a mesh axis runs over, the one named last changes fastest.
Arguments:
- e_field: float32 [6, 16, 64, 512], P('design', None, 'gx', 'gy'), parts along dimension 0, may hold values from -6 to 6
- h_field: float32 [6, 16, 64, 512], P('design', None, 'gx', 'gy'), parts along dimension 0, may hold values from -6 to 6
- inverse_permittivity: float32 [32, 64, 512], P('design', 'gx', 'gy'), parts along dimension 0, may hold values from 0.0833 to 1
- monitor_layer: int32 [128, 512], P(('design', 'gx'), 'gy'), parts along dimension 0, may hold values from 0 to 15
- source_layer: int32 [128, 512], P(('design', 'gx'), 'gy'), parts along dimension 0, may hold values from 0 to 15
- residual_far: float32 [4, 2, 2, 256, 256], P('design', None, None, 'gx', 'gy'), parts along dimension 0, may hold values from -6 to 6
Outputs:
- e_forward: float32 [6, 16, 64, 512], P('design', None, 'gx', 'gy'), parts along dimension 0
- far_field: float32 [4, 2, 2, 256, 256], P('design', None, None, 'gx', 'gy'), parts along dimension 0
- e_adjoint: float32 [6, 16, 64, 512], P('design', None, 'gx', 'gy'), parts along dimension 0
There are 2 independent parts, one for each index of `design`. A program takes and returns all parts, laid end to end along the dimension named above; each array names one. Nothing has to cross between parts.
All inputs are finite; a program needn't handle non-finite values.
Results may differ from a plain program's by a relative error of at most 0.0001.
Values sent between devices are 32-bit elements; how exact they have to be, the bound alone decides.
A program may use at most 64 MiB of HBM per device.

v0:
```python
import math

import jax
import jax.numpy as jnp
from jax import lax
from jax.sharding import PartitionSpec as P

NZ = 16
DIRS = 256


courant = 0.5
omegas = (0.7, 1.3)
factors = (3, 5)
highest = lax.Precision.HIGHEST


def from_behind(value, axis, steps):
    count = lax.axis_size(axis)
    leading, last = (max(0, -steps), min(count, count - steps))
    return lax.ppermute(value, axis, [(source, source + steps) for source in range(leading, last)])


def contract(form, left, right):
    return jnp.einsum(form, left, right, precision=highest)


def ahead(field, along):
    count = field.shape[along]
    widths = [(0, 0)] * field.ndim
    widths[along] = (0, 1)
    return jnp.pad(lax.slice_in_dim(field, 1, count, axis=along), widths)


def behind(field, along):
    count = field.shape[along]
    widths = [(0, 0)] * field.ndim
    widths[along] = (1, 0)
    return jnp.pad(lax.slice_in_dim(field, 0, count - 1, axis=along), widths)


def phase_pair(rows, cols, length):
    cosines = []
    sines = []
    for factor in factors:
        index = jnp.mod((rows[:, None] - DIRS // 2) * cols[None, :] * factor, 4 * length)
        angle = index.astype(jnp.float32) * (2.0 * math.pi / (4 * length))
        cosines.append(jnp.cos(angle))
        sines.append(jnp.sin(angle))
    return (jnp.stack(cosines), jnp.stack(sines))


def step_magnetic(elec, magn):
    face_x = from_behind(jnp.stack([elec[1][:, :1, :], elec[2][:, :1, :]]), "gx", -1)
    face_y = from_behind(jnp.stack([elec[0][:, :, :1], elec[2][:, :, :1]]), "gy", -1)
    next_x1 = jnp.concatenate([elec[1][:, 1:, :], face_x[0]], axis=1)
    next_x2 = jnp.concatenate([elec[2][:, 1:, :], face_x[1]], axis=1)
    next_y0 = jnp.concatenate([elec[0][:, :, 1:], face_y[0]], axis=2)
    next_y2 = jnp.concatenate([elec[2][:, :, 1:], face_y[1]], axis=2)
    curl_x = next_y2 - elec[2] - (ahead(elec[1], 0) - elec[1])
    curl_y = ahead(elec[0], 0) - elec[0] - (next_x2 - elec[2])
    curl_z = next_x1 - elec[1] - (next_y0 - elec[0])
    return magn - courant * jnp.stack([curl_x, curl_y, curl_z])


def step_electric(elec, magn, inverse, current):
    face_x = from_behind(jnp.stack([magn[1][:, -1:, :], magn[2][:, -1:, :]]), "gx", 1)
    face_y = from_behind(jnp.stack([magn[0][:, :, -1:], magn[2][:, :, -1:]]), "gy", 1)
    prev_x1 = jnp.concatenate([face_x[0], magn[1][:, :-1, :]], axis=1)
    prev_x2 = jnp.concatenate([face_x[1], magn[2][:, :-1, :]], axis=1)
    prev_y0 = jnp.concatenate([face_y[0], magn[0][:, :, :-1]], axis=2)
    prev_y2 = jnp.concatenate([face_y[1], magn[2][:, :, :-1]], axis=2)
    curl_x = magn[2] - prev_y2 - (magn[1] - behind(magn[1], 0))
    curl_y = magn[0] - behind(magn[0], 0) - (magn[2] - prev_x2)
    curl_z = magn[1] - prev_x1 - (magn[0] - prev_y0)
    if current is not None:
        curl_x = curl_x - current[0]
        curl_y = curl_y - current[1]
    return elec + courant * inverse[None] * jnp.stack([curl_x, curl_y, curl_z])


def per_device(e_field, h_field, inverse_permittivity, monitor_layer, source_layer, residual_far):
    cells_x = e_field.shape[2]
    cells_y = e_field.shape[3]
    total_x = cells_x * lax.axis_size("gx")
    total_y = cells_y * lax.axis_size("gy")
    global_x = lax.axis_index("gx") * cells_x + jnp.arange(cells_x, dtype=jnp.int32)
    global_y = lax.axis_index("gy") * cells_y + jnp.arange(cells_y, dtype=jnp.int32)
    directions = jnp.arange(DIRS, dtype=jnp.int32)
    elec = e_field
    magn = h_field
    watch = (jnp.arange(NZ, dtype=jnp.int32)[:, None, None] == monitor_layer[None]).astype(
        jnp.float32
    )
    planes = []
    for moment in range(2):
        magn = step_magnetic(elec, magn)
        elec = step_electric(elec, magn, inverse_permittivity, None)
        planes.append(jnp.sum(elec[:2] * watch[None], axis=1))
    e_forward = elec
    spec_real = jnp.stack(
        [math.cos(omega) * planes[0] + math.cos(2 * omega) * planes[1] for omega in omegas]
    )
    spec_imag = jnp.stack(
        [-(math.sin(omega) * planes[0] + math.sin(2 * omega) * planes[1]) for omega in omegas]
    )
    cos_x, sin_x = phase_pair(directions, global_x, total_x)
    cos_y, sin_y = phase_pair(directions, global_y, total_y)
    q_real = contract("fcxy,fby->fcxb", spec_real, cos_y) + contract(
        "fcxy,fby->fcxb", spec_imag, sin_y
    )
    q_imag = contract("fcxy,fby->fcxb", spec_imag, cos_y) - contract(
        "fcxy,fby->fcxb", spec_real, sin_y
    )
    owned = lax.psum_scatter(
        jnp.stack([q_real, q_imag], axis=2), "gy", scatter_dimension=4, tiled=True
    )
    a_real = contract("fax,fcxb->fcab", cos_x, owned[:, :, 0]) + contract(
        "fax,fcxb->fcab", sin_x, owned[:, :, 1]
    )
    a_imag = contract("fax,fcxb->fcab", cos_x, owned[:, :, 1]) - contract(
        "fax,fcxb->fcab", sin_x, owned[:, :, 0]
    )
    summed = lax.psum_scatter(
        jnp.stack([a_real, a_imag], axis=2), "gx", scatter_dimension=3, tiled=True
    )
    far_field = summed * (1.0 / math.sqrt(total_x * total_y))
    piece = lax.all_gather(residual_far, "gy", axis=4, tiled=True)
    rows = jnp.arange(piece.shape[4], dtype=jnp.int32)
    part_cos, part_sin = phase_pair(rows, global_y, total_y)
    u_real = contract("fcab,fby->fcay", piece[:, :, 0], part_cos) - contract(
        "fcab,fby->fcay", piece[:, :, 1], part_sin
    )
    u_imag = contract("fcab,fby->fcay", piece[:, :, 0], part_sin) + contract(
        "fcab,fby->fcay", piece[:, :, 1], part_cos
    )
    mixed = jnp.stack([u_real, u_imag], axis=2)
    piece = lax.all_gather(mixed, "gx", axis=3, tiled=True)
    rows = jnp.arange(piece.shape[3], dtype=jnp.int32)
    part_cos, part_sin = phase_pair(rows, global_x, total_x)
    s_real = contract("fax,fcay->fcxy", part_cos, piece[:, :, 0]) - contract(
        "fax,fcay->fcxy", part_sin, piece[:, :, 1]
    )
    s_imag = contract("fax,fcay->fcxy", part_cos, piece[:, :, 1]) + contract(
        "fax,fcay->fcxy", part_sin, piece[:, :, 0]
    )
    source = jnp.stack([s_real, s_imag], axis=2) / DIRS
    s_real = source[:, :, 0]
    s_imag = source[:, :, 1]
    layers = (jnp.arange(NZ, dtype=jnp.int32)[:, None, None] == source_layer[None]).astype(
        jnp.float32
    )
    elec = jnp.zeros_like(e_field)
    magn = jnp.zeros_like(h_field)
    for moment in range(2):
        tick = moment + 1
        drive = s_real[0] * math.cos(omegas[0] * tick) - s_imag[0] * math.sin(omegas[0] * tick)
        drive = (
            drive + s_real[1] * math.cos(omegas[1] * tick) - s_imag[1] * math.sin(omegas[1] * tick)
        )
        current = layers[None] * drive[:, None]
        magn = step_magnetic(elec, magn)
        elec = step_electric(elec, magn, inverse_permittivity, current)
    return (e_forward, far_field, elec)


def solution(mesh):
    in_specs = (
        P("design", None, "gx", "gy"),
        P("design", None, "gx", "gy"),
        P("design", "gx", "gy"),
        P(("design", "gx"), "gy"),
        P(("design", "gx"), "gy"),
        P("design", None, None, "gx", "gy"),
    )
    out_specs = (
        P("design", None, "gx", "gy"),
        P("design", None, None, "gx", "gy"),
        P("design", None, "gx", "gy"),
    )
    return jax.shard_map(
        per_device, mesh=mesh, in_specs=in_specs, out_specs=out_specs, check_vma=False
    )
```

profile of v0, /device:TPU:0, one launch (start us, length us, event | category | flops | bytes accessed | tf_op | source)
XLA Modules:
  0.0 229.3 jit_solution(10136198741308827661)
XLA Ops:
  15.6 25.8 %all_gather.6 = f32[2,2,2,64,256]{3,2,1,0,4:T(2,128)S(1)} all-gather(f32[2,2,2,64,64]{3,2,1,0,4:T(2,128)S(1)} %copy.993), channel_id=1, replica_groups=mesh['design'=2,'gx'=4,'gy'=4] {'gy'}, dimensions={4}, use_global_device_ids=true | all-gather | bytes 655360 | tf_op jit(solution)/shard_map/all_gather | solution.py:128
  41.5 1.8 fusion.114
  43.3 1.9 copy.1024
  52.5 1.5 collective-permute-start.8
  54.7 1.3 slice_bitcast_fusion
  60.2 1.3 slice.741
  62.6 1.4 copy.1019
  64.0 1.4 copy.1021
  66.0 1.3 slice_bitcast_fusion.63
  69.6 1.5 copy.959
  71.1 4.4 %fusion.9 = (f32[1,16,16,128]{2,1,3,0:T(8,128)}, f32[1,16,16,128]{2,1,3,0:T(8,128)}) fusion(f32[16,16,1]{1,0,2:T(8,128)S(1)} %get-tuple-element.134, f32[16,16,127]{1,0,2:T(8,128)} %slice.737, f32[15,16,128]{1,0,2:T(8,128)} %bitcast.405, f32[1,16,16,128]{2,1,3,0:T(8,128)S(1)} %copy.1020, f32[1,16,16,128]{2,1,3,0:T(8,128)S(1)} %copy.1017, ...), kind=kLoop, calls=%fused_computation.19 | loop fusion | flops 262144 | bytes 1163264 | tf_op jit(solution)/shard_map/stack | solution.py:63
  75.5 1.7 copy.961
  77.6 1.4 copy.960
  79.0 2.9 %fusion.12 = f32[1,16,16,128]{2,1,3,0:T(8,128)} fusion(f32[1,16,16,128]{2,1,3,0:T(8,128)S(1)} %copy.1020, f32[1,16,1,128]{2,1,3,0:T(8,128)} %copy.960, f32[1,16,15,128]{2,1,3,0:T(8,128)S(1)} %copy-done.2, f32[1,16,16,128]{2,1,3,0:T(8,128)S(1)} %copy.1018, f32[1,16,16,1]{2,1,3,0:T(8,128)S(1)} %get-tuple-element.135, f32[1,16,16,127]{2,1,3,0:T(8,128)} %slice_bitcast_fusion.1), kind=kLoop, calls=%fused_computation.24 | loop fusion | flops 163840 | bytes 655360 | tf_op jit(solution)/shard_map/sub | solution.py:62
  81.9 1.7 copy.963
  89.2 1.3 slice_bitcast_fusion.62
  95.7 4.6 %collective-permute-start.2 = (f32[2,16,16,1]{3,2,1,0:T(8,128)S(1)}, f32[2,16,16,1]{3,2,1,0:T(8,128)S(1)}, u32[]{:S(2)}, u32[]{:S(2)}) collective-permute-start(f32[2,16,16,1]{3,2,1,0:T(8,128)S(1)} %copy.964), channel_id=1, source_target_pairs={{0,1},{1,2},{2,3},{4,5},{5,6},{6,7},{8,9},{9,10},{10,11},{12,13},{... | collective-permute-start | bytes 6152 | tf_op jit(solution)/shard_map/ppermute | solution.py:21
  100.3 2.5 %collective-permute-start.3 = (f32[2,16,1,128]{3,1,2,0:T(8,128)S(1)}, f32[2,16,1,128]{3,1,2,0:T(8,128)S(1)}, u32[]{:S(2)}, u32[]{:S(2)}) collective-permute-start(f32[2,16,1,128]{3,1,2,0:T(8,128)S(1)} %pad_maximum_fusion.12), channel_id=1, source_target_pairs={{0,4},{4,8},{8,12},{1,5},{5,9},{9,13},{2,6},{6,10},{10,14},{3,7},{... | collective-permute-start | bytes 49160 | tf_op jit(solution)/shard_map/ppermute | solution.py:21
  103.0 3.0 %collective-permute-start.10 = (f32[2,16,16,1]{3,2,1,0:T(8,128)S(1)}, f32[2,16,16,1]{3,2,1,0:T(8,128)S(1)}, u32[]{:S(2)}, u32[]{:S(2)}) collective-permute-start(f32[2,16,16,1]{3,2,1,0:T(8,128)S(1)} %copy.991), channel_id=1, source_target_pairs={{0,1},{1,2},{2,3},{4,5},{5,6},{6,7},{8,9},{9,10},{10,11},{12,13},{... | collective-permute-start | bytes 6152 | tf_op jit(solution)/shard_map/ppermute | solution.py:21
  106.0 4.0 %collective-permute-start.11 = (f32[2,16,1,128]{3,1,2,0:T(8,128)S(1)}, f32[2,16,1,128]{3,1,2,0:T(8,128)S(1)}, u32[]{:S(2)}, u32[]{:S(2)}) collective-permute-start(f32[2,16,1,128]{3,1,2,0:T(8,128)S(1)} %pad_maximum_fusion.18), channel_id=1, source_target_pairs={{0,4},{4,8},{8,12},{1,5},{5,9},{9,13},{2,6},{6,10},{10,14},{3,7},{... | collective-permute-start | bytes 49160 | tf_op jit(solution)/shard_map/ppermute | solution.py:21
  114.1 1.4 fusion.13
  115.5 1.4 fusion.14
  128.8 5.1 %collective-permute-done.4 = f32[2,16,16,1]{3,2,1,0:T(8,128)} collective-permute-done((f32[2,16,16,1]{3,2,1,0:T(8,128)}, f32[2,16,16,1]{3,2,1,0:T(8,128)}, u32[]{:S(2)}, u32[]{:S(2)}) %collective-permute-start.4) | collective-permute-done | bytes 2080 | tf_op jit(solution)/shard_map/ppermute | solution.py:21
  134.9 4.5 %collective-permute-done.12 = f32[2,16,16,1]{3,2,1,0:T(8,128)S(1)} collective-permute-done((f32[2,16,16,1]{3,2,1,0:T(8,128)}, f32[2,16,16,1]{3,2,1,0:T(8,128)S(1)}, u32[]{:S(2)}, u32[]{:S(2)}) %collective-permute-start.12) | collective-permute-done | bytes 2080 | tf_op jit(solution)/shard_map/ppermute | solution.py:21
  147.6 4.8 %collective-permute-start.6 = (f32[2,16,16,1]{3,2,1,0:T(8,128)S(1)}, f32[2,16,16,1]{3,2,1,0:T(8,128)}, u32[]{:S(2)}, u32[]{:S(2)}) collective-permute-start(f32[2,16,16,1]{3,2,1,0:T(8,128)S(1)} %copy.972), channel_id=1, source_target_pairs={{0,1},{1,2},{2,3},{4,5},{5,6},{6,7},{8,9},{9,10},{10,11},{12,13},{... | collective-permute-start | bytes 6152 | tf_op jit(solution)/shard_map/ppermute | solution.py:21
  153.1 2.4 %collective-permute-start.7 = (f32[2,16,1,128]{3,1,2,0:T(8,128)}, f32[2,16,1,128]{3,1,2,0:T(8,128)}, u32[]{:S(2)}, u32[]{:S(2)}) collective-permute-start(f32[2,16,1,128]{3,1,2,0:T(8,128)} %pad_maximum_fusion.16), channel_id=1, source_target_pairs={{0,4},{4,8},{8,12},{1,5},{5,9},{9,13},{2,6},{6,10},{10,14},{3,7},{... | collective-permute-start | bytes 49160 | tf_op jit(solution)/shard_map/ppermute | solution.py:21
  156.4 3.5 %collective-permute-start.14 = (f32[2,16,16,1]{3,2,1,0:T(8,128)}, f32[2,16,16,1]{3,2,1,0:T(8,128)S(1)}, u32[]{:S(2)}, u32[]{:S(2)}) collective-permute-start(f32[2,16,16,1]{3,2,1,0:T(8,128)} %copy.1002), channel_id=1, source_target_pairs={{0,1},{1,2},{2,3},{4,5},{5,6},{6,7},{8,9},{9,10},{10,11},{12,13},{... | collective-permute-start | bytes 6152 | tf_op jit(solution)/shard_map/ppermute | solution.py:21
  159.9 4.3 %collective-permute-start.15 = (f32[2,16,1,128]{3,1,2,0:T(8,128)S(1)}, f32[2,16,1,128]{3,1,2,0:T(8,128)S(1)}, u32[]{:S(2)}, u32[]{:S(2)}) collective-permute-start(f32[2,16,1,128]{3,1,2,0:T(8,128)S(1)} %pad_maximum_fusion.22), channel_id=1, source_target_pairs={{0,4},{4,8},{8,12},{1,5},{5,9},{9,13},{2,6},{6,10},{10,14},{3,7},{... | collective-permute-start | bytes 49160 | tf_op jit(solution)/shard_map/ppermute | solution.py:21
  172.1 1.9 reshape.781
  174.2 19.9 %reduce-scatter.7.cloned.1.call-done = f32[64,128]{1,0:T(8,128)} async-done(((f32[256,128]{1,0:T(8,128)}), f32[64,128]{1,0:T(8,128)}) %reduce-scatter.7.cloned.1.call-update) | async-done | bytes 32784
  198.9 1.7 reshape.783
  200.6 20.0 %reduce-scatter.9.cloned.1.call-done = f32[64,512]{1,0:T(8,128)} async-done(((f32[256,512]{1,0:T(8,128)}), f32[64,512]{1,0:T(8,128)}) %reduce-scatter.9.cloned.1.call-update) | async-done | bytes 131088
  (319 shorter events, 76.5 us)
Async XLA Ops:
  7.2 106.3 %all-gather.2.cloned.1.call-start = ((), (), s32[]{:S(2)}) async-start(), calls=%async_computation.2 | async-start | bytes 1310720 | tf_op jit(solution)/shard_map/all_gather | solution.py:138
  9.9 57.5 %collective-permute-start = (f32[2,16,16,1]{2,1,3,0:T(8,128)}, f32[2,16,16,1]{2,1,3,0:T(8,128)}, u32[]{:S(2)}, u32[]{:S(2)}) collective-permute-start(f32[2,16,16,1]{2,1,3,0:T(8,128)} %pad_maximum_fusion.9), channel_id=1, source_target_pairs={{1,0},{2,1},{3,2},{5,4},{6,5},{7,6},{9,8},{10,9},{11,10},{13,12},{... | collective-permute-start | bytes 6152 | tf_op jit(solution)/shard_map/ppermute | solution.py:21
  13.1 55.7 %collective-permute-start.1 = (f32[2,16,1,128]{3,1,2,0:T(8,128)}, f32[2,16,1,128]{3,1,2,0:T(8,128)}, u32[]{:S(2)}, u32[]{:S(2)}) collective-permute-start(f32[2,16,1,128]{3,1,2,0:T(8,128)} %pad_maximum_fusion.10), channel_id=1, source_target_pairs={{4,0},{8,4},{12,8},{5,1},{9,5},{13,9},{6,2},{10,6},{14,10},{7,3},{... | collective-permute-start | bytes 49160 | tf_op jit(solution)/shard_map/ppermute | solution.py:21
  14.5 31.9 %copy-start.59 = (s32[256]{0:T(256)}, s32[256]{0:T(256)S(1)}, u32[]{:S(2)}) copy-start(s32[256]{0:T(256)S(1)} %iota_add_fusion) | copy-start | bytes 3076
  49.2 4.8 %copy-start.11 = (f32[3,16,16,128]{3,2,1,0:T(8,128)S(1)}, f32[3,16,16,128]{3,2,1,0:T(8,128)}, u32[]{:S(2)}) copy-start(f32[3,16,16,128]{3,2,1,0:T(8,128)} %param.6) | copy-start | bytes 1179652
  50.0 144.1 %reduce-scatter.7.cloned.1.call-start = ((), (), s32[]{:S(2)}) async-start(), calls=%async_computation.3 | async-start | bytes 163840
  50.6 38.5 %collective-permute-start.9 = (f32[2,16,1,128]{3,1,2,0:T(8,128)}, f32[2,16,1,128]{3,1,2,0:T(8,128)}, u32[]{:S(2)}, u32[]{:S(2)}) collective-permute-start(f32[2,16,1,128]{3,1,2,0:T(8,128)} %stack.342), channel_id=1, source_target_pairs={{4,0},{8,4},{12,8},{5,1},{9,5},{13,9},{6,2},{10,6},{14,10},{7,3},{... | collective-permute-start | bytes 49160 | tf_op jit(solution)/shard_map/ppermute | solution.py:21
  52.5 13.5 %collective-permute-start.8 = (f32[2,16,16,1]{2,1,3,0:T(8,128)}, f32[2,16,16,1]{2,1,3,0:T(8,128)}, u32[]{:S(2)}, u32[]{:S(2)}) collective-permute-start(f32[2,16,16,1]{2,1,3,0:T(8,128)} %stack.340), channel_id=1, source_target_pairs={{1,0},{2,1},{3,2},{5,4},{6,5},{7,6},{9,8},{10,9},{11,10},{13,12},{... | collective-permute-start | bytes 6152 | tf_op jit(solution)/shard_map/ppermute | solution.py:21
  77.2 6.4 %copy-start.18 = (f32[1,16,16,128]{3,2,1,0:T(8,128)}, f32[1,16,16,128]{3,2,1,0:T(8,128)S(1)}, u32[]{:S(2)}) copy-start(f32[1,16,16,128]{3,2,1,0:T(8,128)S(1)} %copy.961) | copy-start | bytes 393220
  77.6 6.0 %copy-start.20 = (f32[1,16,16,128]{3,2,1,0:T(8,128)}, f32[1,16,16,128]{3,2,1,0:T(8,128)S(1)}, u32[]{:S(2)}) copy-start(f32[1,16,16,128]{3,2,1,0:T(8,128)S(1)} %copy.962) | copy-start | bytes 393220
  84.3 3.6 %copy-start.14 = (f32[16,16,128]{2,1,0:T(8,128)}, f32[16,16,128]{2,1,0:T(8,128)S(1)}, u32[]{:S(2)}) copy-start(f32[16,16,128]{2,1,0:T(8,128)S(1)} %get-tuple-element.86) | copy-start | bytes 393220
  95.4 4.8 %copy-start.53 = (f32[16,1,128]{2,1,0:T(1,128)S(1)}, f32[16,1,128]{2,1,0:T(1,128)}, u32[]{:S(2)}) copy-start(f32[16,1,128]{2,1,0:T(1,128)} %slice.759) | copy-start | bytes 24580
  95.4 4.8 %copy-start.54 = (f32[16,1,128]{2,1,0:T(1,128)S(1)}, f32[16,1,128]{2,1,0:T(1,128)}, u32[]{:S(2)}) copy-start(f32[16,1,128]{2,1,0:T(1,128)} %slice.758) | copy-start | bytes 24580
  95.7 14.4 %collective-permute-start.2 = (f32[2,16,16,1]{3,2,1,0:T(8,128)S(1)}, f32[2,16,16,1]{3,2,1,0:T(8,128)S(1)}, u32[]{:S(2)}, u32[]{:S(2)}) collective-permute-start(f32[2,16,16,1]{3,2,1,0:T(8,128)S(1)} %copy.964), channel_id=1, source_target_pairs={{0,1},{1,2},{2,3},{4,5},{5,6},{6,7},{8,9},{9,10},{10,11},{12,13},{... | collective-permute-start | bytes 6152 | tf_op jit(solution)/shard_map/ppermute | solution.py:21
  100.3 11.0 %collective-permute-start.3 = (f32[2,16,1,128]{3,1,2,0:T(8,128)S(1)}, f32[2,16,1,128]{3,1,2,0:T(8,128)S(1)}, u32[]{:S(2)}, u32[]{:S(2)}) collective-permute-start(f32[2,16,1,128]{3,1,2,0:T(8,128)S(1)} %pad_maximum_fusion.12), channel_id=1, source_target_pairs={{0,4},{4,8},{8,12},{1,5},{5,9},{9,13},{2,6},{6,10},{10,14},{3,7},{... | collective-permute-start | bytes 49160 | tf_op jit(solution)/shard_map/ppermute | solution.py:21
  103.0 8.2 %collective-permute-start.10 = (f32[2,16,16,1]{3,2,1,0:T(8,128)S(1)}, f32[2,16,16,1]{3,2,1,0:T(8,128)S(1)}, u32[]{:S(2)}, u32[]{:S(2)}) collective-permute-start(f32[2,16,16,1]{3,2,1,0:T(8,128)S(1)} %copy.991), channel_id=1, source_target_pairs={{0,1},{1,2},{2,3},{4,5},{5,6},{6,7},{8,9},{9,10},{10,11},{12,13},{... | collective-permute-start | bytes 6152 | tf_op jit(solution)/shard_map/ppermute | solution.py:21
  106.0 5.2 %collective-permute-start.11 = (f32[2,16,1,128]{3,1,2,0:T(8,128)S(1)}, f32[2,16,1,128]{3,1,2,0:T(8,128)S(1)}, u32[]{:S(2)}, u32[]{:S(2)}) collective-permute-start(f32[2,16,1,128]{3,1,2,0:T(8,128)S(1)} %pad_maximum_fusion.18), channel_id=1, source_target_pairs={{0,4},{4,8},{8,12},{1,5},{5,9},{9,13},{2,6},{6,10},{10,14},{3,7},{... | collective-permute-start | bytes 49160 | tf_op jit(solution)/shard_map/ppermute | solution.py:21
  113.5 3.5 %copy-start.1 = (f32[2,2,2,256,128]{4,3,1,0,2:T(8,128)S(1)}, f32[2,2,2,256,128]{4,3,1,0,2:T(8,128)}, u32[]{:S(2)}) copy-start(f32[2,2,2,256,128]{4,3,1,0,2:T(8,128)} %all-gather.2.cloned.1.call-done) | copy-start | bytes 3145732
  122.6 11.3 %collective-permute-start.4 = (f32[2,16,16,1]{3,2,1,0:T(8,128)}, f32[2,16,16,1]{3,2,1,0:T(8,128)}, u32[]{:S(2)}, u32[]{:S(2)}) collective-permute-start(f32[2,16,16,1]{3,2,1,0:T(8,128)} %copy.968), channel_id=1, source_target_pairs={{1,0},{2,1},{3,2},{5,4},{6,5},{7,6},{9,8},{10,9},{11,10},{13,12},{... | collective-permute-start | bytes 6152 | tf_op jit(solution)/shard_map/ppermute | solution.py:21
  123.9 15.5 %collective-permute-start.5 = (f32[2,16,1,128]{3,1,2,0:T(8,128)S(1)}, f32[2,16,1,128]{3,1,2,0:T(8,128)S(1)}, u32[]{:S(2)}, u32[]{:S(2)}) collective-permute-start(f32[2,16,1,128]{3,1,2,0:T(8,128)S(1)} %pad_maximum_fusion.14), channel_id=1, source_target_pairs={{4,0},{8,4},{12,8},{5,1},{9,5},{13,9},{6,2},{10,6},{14,10},{7,3},{... | collective-permute-start | bytes 49160 | tf_op jit(solution)/shard_map/ppermute | solution.py:21
  126.2 13.2 %collective-permute-start.12 = (f32[2,16,16,1]{3,2,1,0:T(8,128)}, f32[2,16,16,1]{3,2,1,0:T(8,128)S(1)}, u32[]{:S(2)}, u32[]{:S(2)}) collective-permute-start(f32[2,16,16,1]{3,2,1,0:T(8,128)} %copy.998), channel_id=1, source_target_pairs={{1,0},{2,1},{3,2},{5,4},{6,5},{7,6},{9,8},{10,9},{11,10},{13,12},{... | collective-permute-start | bytes 6152 | tf_op jit(solution)/shard_map/ppermute | solution.py:21
  127.5 15.6 %collective-permute-start.13 = (f32[2,16,1,128]{3,1,2,0:T(8,128)S(1)}, f32[2,16,1,128]{3,1,2,0:T(8,128)S(1)}, u32[]{:S(2)}, u32[]{:S(2)}) collective-permute-start(f32[2,16,1,128]{3,1,2,0:T(8,128)S(1)} %pad_maximum_fusion.20), channel_id=1, source_target_pairs={{4,0},{8,4},{12,8},{5,1},{9,5},{13,9},{6,2},{10,6},{14,10},{7,3},{... | collective-permute-start | bytes 49160 | tf_op jit(solution)/shard_map/ppermute | solution.py:21
  147.3 5.1 %copy-start.51 = (f32[16,1,128]{2,1,0:T(1,128)S(1)}, f32[16,1,128]{2,1,0:T(1,128)}, u32[]{:S(2)}) copy-start(f32[16,1,128]{2,1,0:T(1,128)} %slice.792) | copy-start | bytes 24580
  147.3 5.1 %copy-start.52 = (f32[16,1,128]{2,1,0:T(1,128)S(1)}, f32[16,1,128]{2,1,0:T(1,128)}, u32[]{:S(2)}) copy-start(f32[16,1,128]{2,1,0:T(1,128)} %slice.793) | copy-start | bytes 24580
  147.6 16.7 %collective-permute-start.6 = (f32[2,16,16,1]{3,2,1,0:T(8,128)S(1)}, f32[2,16,16,1]{3,2,1,0:T(8,128)}, u32[]{:S(2)}, u32[]{:S(2)}) collective-permute-start(f32[2,16,16,1]{3,2,1,0:T(8,128)S(1)} %copy.972), channel_id=1, source_target_pairs={{0,1},{1,2},{2,3},{4,5},{5,6},{6,7},{8,9},{9,10},{10,11},{12,13},{... | collective-permute-start | bytes 6152 | tf_op jit(solution)/shard_map/ppermute | solution.py:21
  152.4 3.0 %copy-start.49 = (f32[16,16]{1,0:T(8,128)S(1)}, f32[16,16]{1,0:T(8,128)}, u32[]{:S(2)}) copy-start(f32[16,16]{1,0:T(8,128)} %slice_reduce_fusion.1) | copy-start | bytes 3076
  153.1 12.3 %collective-permute-start.7 = (f32[2,16,1,128]{3,1,2,0:T(8,128)}, f32[2,16,1,128]{3,1,2,0:T(8,128)}, u32[]{:S(2)}, u32[]{:S(2)}) collective-permute-start(f32[2,16,1,128]{3,1,2,0:T(8,128)} %pad_maximum_fusion.16), channel_id=1, source_target_pairs={{0,4},{4,8},{8,12},{1,5},{5,9},{9,13},{2,6},{6,10},{10,14},{3,7},{... | collective-permute-start | bytes 49160 | tf_op jit(solution)/shard_map/ppermute | solution.py:21
  155.4 4.5 %copy-start.55 = (f32[16,1,128]{2,1,0:T(1,128)S(1)}, f32[16,1,128]{2,1,0:T(1,128)}, u32[]{:S(2)}) copy-start(f32[16,1,128]{2,1,0:T(1,128)} %slice.863) | copy-start | bytes 24580
  155.4 4.5 %copy-start.56 = (f32[16,1,128]{2,1,0:T(1,128)S(1)}, f32[16,1,128]{2,1,0:T(1,128)}, u32[]{:S(2)}) copy-start(f32[16,1,128]{2,1,0:T(1,128)} %slice.862) | copy-start | bytes 24580
  156.4 8.9 %collective-permute-start.14 = (f32[2,16,16,1]{3,2,1,0:T(8,128)}, f32[2,16,16,1]{3,2,1,0:T(8,128)S(1)}, u32[]{:S(2)}, u32[]{:S(2)}) collective-permute-start(f32[2,16,16,1]{3,2,1,0:T(8,128)} %copy.1002), channel_id=1, source_target_pairs={{0,1},{1,2},{2,3},{4,5},{5,6},{6,7},{8,9},{9,10},{10,11},{12,13},{... | collective-permute-start | bytes 6152 | tf_op jit(solution)/shard_map/ppermute | solution.py:21
  159.9 6.2 %collective-permute-start.15 = (f32[2,16,1,128]{3,1,2,0:T(8,128)S(1)}, f32[2,16,1,128]{3,1,2,0:T(8,128)S(1)}, u32[]{:S(2)}, u32[]{:S(2)}) collective-permute-start(f32[2,16,1,128]{3,1,2,0:T(8,128)S(1)} %pad_maximum_fusion.22), channel_id=1, source_target_pairs={{0,4},{4,8},{8,12},{1,5},{5,9},{9,13},{2,6},{6,10},{10,14},{3,7},{... | collective-permute-start | bytes 49160 | tf_op jit(solution)/shard_map/ppermute | solution.py:21
  174.1 46.5 %reduce-scatter.9.cloned.1.call-start = ((), (), s32[]{:S(2)}) async-start(), calls=%async_computation.4 | async-start | bytes 655360
  (49 other events, 48.1 us)
Sparse Core Ops, SparseCore 0:
  50.1 18.6 all-gather.1
  174.2 19.7 reduce-scatter.6
  200.7 19.8 reduce-scatter.8
where the time goes:
time: 231 us; the launch traced here: 229 us
  local copies, waits for them, and re-layouts  71.8 us (31%)
  waiting for transfers between devices  50.7 us (22%)
  starting transfers between devices  39.6 us (17%)
  blocking collectives  25.8 us (11%)
  other arithmetic  17.8 us (8%)
  between operations  15.1 us (7%)
  matrix products  8.31 us (4%)
    unnamed x5, waiting for transfers between devices  39.9 us
    ppermute x16, starting transfers between devices, from_behind(): lax.ppermute(value, axis, [(source, source + steps) for source in range(l...  39.5 us
    unnamed x142, local copies, waits for them, and re-layouts  30 us
    all_gather x1, blocking collectives, per_device(): piece = lax.all_gather(residual_far, 'gy', axis=4, tiled=True)  25.8 us
    ppermute x16, waiting for transfers between devices, from_behind(): lax.ppermute(value, axis, [(source, source + steps) for source in range(l...  10.8 us
    dot_general x16, matrix products, contract(): return jnp.einsum(form, left, right, precision=highest)  8.31 us
    another operation x5, other arithmetic, step_magnetic(): return magn - courant * jnp.stack([curl_x, curl_y, curl_z])  5.85 us
  transfers between devices with their start and end apart: 19, of which 5 were waited for; matrix products, arithmetic and copies ran while one was open for 26% of the time, Pallas kernels for 0%

commit v1 on v0

v1 whole, which is shorter than its diff:
```python
import functools
import math

import jax
import jax.numpy as jnp
import ml_dtypes
import numpy as np
from jax import lax
from jax.experimental import pallas as pl
from jax.experimental.pallas import tpu as pltpu
from jax.sharding import PartitionSpec as P

courant = 0.5
omegas = (0.7, 1.3)
factors = (3, 5)
MESH = pl.DeviceIdType.MESH
ticks = (1, 2)


def halves(table):
    high = table.astype(ml_dtypes.bfloat16)
    low = (table - high.astype(np.float64)).astype(ml_dtypes.bfloat16)
    return np.stack([high, low], axis=-3)


def angles(dirs, length):
    rows = np.arange(dirs)[:, None] - dirs // 2
    cols = np.arange(length)[None, :]
    return np.stack(
        [np.mod(rows * cols * factor, 4 * length) * (2.0 * np.pi / (4 * length)) for factor in factors]
    )


def tables(gx, gy, na, nb, nx, ny):
    theta = angles(gx * na, gx * nx)
    phi = angles(gy * nb, gy * ny)
    freqs = len(factors)
    shifted = np.stack([phi + np.array(omegas)[:, None, None] * t for t in ticks])
    both = np.stack([np.cos(shifted), -np.sin(shifted)], axis=2)
    both = both.reshape(len(ticks), freqs, 2, gy, nb, gy, ny)
    far_y = both.transpose(3, 0, 5, 6, 1, 2, 4).reshape(gy, len(ticks), gy, ny, freqs * 2 * nb)
    back_y = both.transpose(5, 3, 1, 2, 4, 0, 6).reshape(gy, gy, freqs, 2 * nb, len(ticks) * ny)
    back_y = back_y / (gx * na)
    pair = np.stack([np.cos(theta), np.sin(theta)], axis=1).reshape(freqs, 2, gx, na, gx * nx)
    far_x = pair.transpose(2, 0, 1, 3, 4).reshape(gx, freqs, 2 * na, gx * nx)
    far_x = far_x / math.sqrt(gx * nx * gy * ny)
    cos, sin = np.cos(theta), np.sin(theta)
    mix = np.stack([np.stack([cos, -sin]), np.stack([sin, cos])])
    mix = mix.reshape(2, 2, freqs, gx, na, gx, nx)
    back_x = mix.transpose(3, 2, 5, 0, 6, 1, 4).reshape(gx, freqs, gx * 2 * nx, 2 * na)
    return halves(far_y), halves(back_y), halves(far_x), halves(back_x)


def split(value):
    high = value.astype(jnp.bfloat16)
    return high, (value - high.astype(jnp.float32)).astype(jnp.bfloat16)


def mul(left, right):
    return jnp.dot(left, right, preferred_element_type=jnp.float32)


def triple(left, right):
    return mul(left[0], right[0]) + (mul(left[0], right[1]) + mul(left[1], right[0]))


def kernel(
    gx, gy,
    e_in, h_in, k_in, mon_in, src_in, res_in, far_y_in, back_y_in, far_x_in, back_x_in,
    e_out, far_out, adj_out,
    elec, magn, inv, mon, src, res, far_y, back_y, far_x, back_x,
    aelec, amagn, afinal, far,
    row_send, col_send, row_recv, col_recv,
    vsend, vrecv, vall, planes, qall,
    in_sems, out_sems, halo_send, halo_recv, v_send, v_recv, g_send, g_recv, p_send, p_recv, q_send, q_recv,
):
    mx = lax.axis_index("gx")
    my = lax.axis_index("gy")
    _, nz, nx, ny = e_in.shape
    na, nb = res_in.shape[3:]
    freqs = len(factors)

    loads = {}
    for slot, (name, source, target) in enumerate((
        ("res", res_in, res),
        ("back_x", back_x_in.at[mx], back_x),
        ("e", e_in, elec.at[:, pl.ds(0, nz)]),
        ("h", h_in, magn.at[:, pl.ds(1, nz)]),
        ("k", k_in, inv),
        ("mon", mon_in, mon),
        ("src", src_in, src),
        ("back_y", back_y_in.at[my], back_y),
        ("far_y", far_y_in.at[my], far_y),
        ("far_x", far_x_in.at[mx], far_x),
    )):
        loads[name] = pltpu.make_async_copy(source, target, in_sems.at[slot])
        loads[name].start()

    row_recv[...] = jnp.zeros_like(row_recv)
    col_recv[...] = jnp.zeros_like(col_recv)
    blank = jnp.zeros((nx, ny), jnp.float32)
    for part in range(3):
        elec[part, nz] = blank
        magn[part, 0] = blank
        amagn[part, 0] = blank
    for part in range(2):
        aelec[part, nz] = blank

    barrier = pltpu.get_barrier_semaphore()
    for step in range(1, gx):
        pl.semaphore_signal(barrier, inc=1, device_id={"gx": lax.rem(mx + step, gx)}, device_id_type=MESH)
    for step in range(1, gy):
        pl.semaphore_signal(barrier, inc=1, device_id={"gy": lax.rem(my + step, gy)}, device_id_type=MESH)

    lanes = lax.broadcasted_iota(jnp.int32, (nx, ny), 1)
    rows = lax.broadcasted_iota(jnp.int32, (nx, ny), 0)

    def each_z(body, init):
        return lax.fori_loop(0, nz, body, init, unroll=True)

    def ahead_x(value, edge):
        return jnp.where(rows == nx - 1, edge, pltpu.roll(value, nx - 1, axis=0))

    def behind_x(value, edge):
        return jnp.where(rows == 0, edge, pltpu.roll(value, 1, axis=0))

    def ahead_y(value, packed, lane):
        edge = pltpu.roll(packed, lax.rem(2 * ny - 1 - lane, ny), axis=1)
        return jnp.where(lanes == ny - 1, edge, pltpu.roll(value, ny - 1, axis=1))

    def behind_y(value, packed, lane):
        edge = pltpu.roll(packed, lax.rem(2 * ny - lane, ny), axis=1)
        return jnp.where(lanes == 0, edge, pltpu.roll(value, 1, axis=1))

    def pack_first(value, lane, packed):
        return jnp.where(lanes == lane, pltpu.roll(value, lane, axis=1), packed)

    def pack_last(value, lane, packed):
        return jnp.where(lanes == lane, pltpu.roll(value, lane + 1, axis=1), packed)

    def halo(number, direction, count):
        size = gx, gy
        place = mx, my
        out = []
        for which, (axis, send, recv) in enumerate((("gx", row_send, row_recv), ("gy", col_send, col_recv))):
            here, total = place[which], size[which]
            target = lax.rem(here + direction + total, total)
            source_ref = send.at[number, pl.ds(0, count)] if which == 0 else send.at[number]
            target_ref = recv.at[number, pl.ds(0, count)] if which == 0 else recv.at[number]
            copy = pltpu.make_async_remote_copy(
                src_ref=source_ref,
                dst_ref=target_ref,
                send_sem=halo_send.at[number, which],
                recv_sem=halo_recv.at[number, which],
                device_id={axis: target},
                device_id_type=MESH,
            )
            sends = here >= 1 if direction < 0 else here < total - 1
            takes = here < total - 1 if direction < 0 else here >= 1
            out.append((copy, sends, takes))
        return out

    halos = [halo(number, direction, count) for number, (direction, count) in enumerate(
        ((-1, 2), (1, 2), (-1, 2), (1, 2), (-1, 1), (1, 2)))]

    def send_halo(number):
        for copy, sends, _ in halos[number]:
            pl.when(sends)(copy.start)

    def take_halo(number):
        for copy, _, takes in halos[number]:
            pl.when(takes)(copy.wait_recv)

    def end_halo(number):
        for copy, sends, _ in halos[number]:
            pl.when(sends)(copy.wait_send)

    def spread(axis, source, target, send, recv):
        here, total = (mx, gx) if axis == "gx" else (my, gy)
        out = []
        for step in range(1, total):
            other = lax.rem(here + step, total)
            out.append((
                pltpu.make_async_remote_copy(
                    src_ref=source(other), dst_ref=target(here),
                    send_sem=send(other), recv_sem=recv(here),
                    device_id={axis: other}, device_id_type=MESH),
                pltpu.make_async_remote_copy(
                    src_ref=source(other), dst_ref=target(other),
                    send_sem=send(other), recv_sem=recv(other),
                    device_id={axis: other}, device_id_type=MESH),
            ))
        return out

    def start(copies):
        for copy, _ in copies:
            copy.start()

    def arrive(copies):
        for _, copy in copies:
            copy.wait_recv()

    def left(copies):
        for copy, _ in copies:
            copy.wait_send()

    loads["res"].wait()
    loads["back_x"].wait()
    for f in range(freqs):
        block = jnp.concatenate(
            [jnp.concatenate([res[f, c, 0], res[f, c, 1]], axis=0) for c in range(2)], axis=1)
        part = triple((back_x[f, 0], back_x[f, 1]), split(block))
        for other in range(gx):
            vsend[other, f] = part[other * 2 * nx:(other + 1) * 2 * nx]

    loads["e"].wait()

    def pack_start(z, packed):
        row_send[0, 0, pl.ds(z, 1)] = elec[1, z, 0:1]
        row_send[0, 1, pl.ds(z, 1)] = elec[2, z, 0:1]
        packed = pack_first(elec[0, z], z, packed)
        return pack_first(elec[2, z], nz + z, packed)

    col_send[0] = each_z(pack_start, blank)
    pl.semaphore_wait(barrier, gx - 1 + gy - 1)
    send_halo(0)
    v_copies = spread("gx", lambda other: vsend.at[other], lambda slot: vrecv.at[slot],
                      lambda other: v_send.at[other], lambda slot: v_recv.at[slot])
    start(v_copies)

    def magnetic(number, after):
        def body(z, packed):
            ex, ey, ez = elec[0, z], elec[1, z], elec[2, z]
            x_face = row_recv.at[number]
            next_x1 = ahead_x(ey, x_face[0, pl.ds(z, 1)])
            next_x2 = ahead_x(ez, x_face[1, pl.ds(z, 1)])
            cols = col_recv[number]
            next_y0 = ahead_y(ex, cols, z)
            next_y2 = ahead_y(ez, cols, nz + z)
            hx = magn[0, z + 1] - courant * ((next_y2 - ez) - (elec[1, z + 1] - ey))
            hy = magn[1, z + 1] - courant * ((elec[0, z + 1] - ex) - (next_x2 - ez))
            hz = magn[2, z + 1] - courant * ((next_x1 - ey) - (next_y0 - ex))
            magn[0, z + 1] = hx
            magn[1, z + 1] = hy
            magn[2, z + 1] = hz
            row_send[after, 0, pl.ds(z, 1)] = hy[nx - 1:nx]
            row_send[after, 1, pl.ds(z, 1)] = hz[nx - 1:nx]
            return pack_last(hz, nz + z, pack_last(hx, z, packed))
        col_send[after] = each_z(body, blank)

    def curls(field, number, z):
        hx, hy, hz = field[0, z + 1], field[1, z + 1], field[2, z + 1]
        x_face = row_recv.at[number]
        prev_x1 = behind_x(hy, x_face[0, pl.ds(z, 1)])
        prev_x2 = behind_x(hz, x_face[1, pl.ds(z, 1)])
        cols = col_recv[number]
        prev_y0 = behind_y(hx, cols, z)
        prev_y2 = behind_y(hz, cols, nz + z)
        curl_x = (hz - prev_y2) - (hy - field[1, z])
        curl_y = (hx - field[0, z]) - (hz - prev_x2)
        curl_z = (hy - prev_x1) - (hx - prev_y0)
        return curl_x, curl_y, curl_z

    def electric(number, after, tick):
        def body(z, carry):
            packed, plane_x, plane_y = carry
            gain = courant * inv[z]
            curl_x, curl_y, curl_z = curls(magn, number, z)
            ex = elec[0, z] + gain * curl_x
            ey = elec[1, z] + gain * curl_y
            ez = elec[2, z] + gain * curl_z
            elec[0, z] = ex
            elec[1, z] = ey
            elec[2, z] = ez
            seen = mon[...] == z
            plane_x = jnp.where(seen, ex, plane_x)
            plane_y = jnp.where(seen, ey, plane_y)
            if after is not None:
                row_send[after, 0, pl.ds(z, 1)] = ey[0:1]
                row_send[after, 1, pl.ds(z, 1)] = ez[0:1]
                packed = pack_first(ez, nz + z, pack_first(ex, z, packed))
            return packed, plane_x, plane_y
        packed, plane_x, plane_y = each_z(body, (blank, blank, blank))
        if after is not None:
            col_send[after] = packed
        planes[tick, my, 0:nx] = plane_x
        planes[tick, my, nx:2 * nx] = plane_y

    def plane_copies(tick):
        return spread("gy", lambda other: planes.at[tick, my], lambda slot: planes.at[tick, slot],
                      lambda other: p_send.at[tick, other], lambda slot: p_recv.at[tick, slot])

    first_planes, second_planes = plane_copies(0), plane_copies(1)
    g_copies = spread("gy", lambda other: vall.at[my], lambda slot: vall.at[slot],
                      lambda other: g_send.at[other], lambda slot: g_recv.at[slot])
    q_copies = spread("gx", lambda other: qall.at[:, mx], lambda slot: qall.at[:, slot],
                      lambda other: q_send.at[other], lambda slot: q_recv.at[slot])

    loads["h"].wait()
    take_halo(0)
    magnetic(0, 1)
    send_halo(1)

    arrive(v_copies)
    vrecv[mx] = vsend[mx]
    for f in range(freqs):
        total = vrecv[0, f]
        for slot in range(1, gx):
            total = total + vrecv[slot, f]
        top, low = total[0:nx], total[nx:2 * nx]
        for c in range(2):
            vall[my, f, c * nx:(c + 1) * nx] = jnp.concatenate(
                [top[:, c * nb:(c + 1) * nb], low[:, c * nb:(c + 1) * nb]], axis=1)
    start(g_copies)

    for name in ("k", "mon", "src"):
        loads[name].wait()
    take_halo(1)
    electric(1, 2, 0)
    send_halo(2)
    start(first_planes)

    take_halo(2)
    magnetic(2, 3)
    send_halo(3)

    arrive(g_copies)
    loads["back_y"].wait()
    drive = jnp.zeros((2 * nx, len(ticks) * ny), jnp.float32)
    for slot in range(gy):
        for f in range(freqs):
            drive = drive + triple(split(vall[slot, f]), (back_y[slot, f, 0], back_y[slot, f, 1]))

    def adjoint_first(z, packed):
        lit = jnp.where(src[...] == z, (-courant) * inv[z], 0.0)
        ex = lit * drive[0:nx, 0:ny]
        ey = lit * drive[nx:2 * nx, 0:ny]
        aelec[0, z] = ex
        aelec[1, z] = ey
        row_send[4, 0, pl.ds(z, 1)] = ey[0:1]
        return pack_first(ex, z, packed)

    col_send[4] = each_z(adjoint_first, blank)
    send_halo(4)

    take_halo(3)
    electric(3, None, 1)
    start(second_planes)
    stores = [pltpu.make_async_copy(elec.at[:, pl.ds(0, nz)], e_out, out_sems.at[0])]
    stores[0].start()

    take_halo(4)

    def adjoint_magnetic(z, packed):
        ex, ey = aelec[0, z], aelec[1, z]
        next_x1 = ahead_x(ey, row_recv[4, 0, pl.ds(z, 1)])
        next_y0 = ahead_y(ex, col_recv[4], z)
        hx = courant * (aelec[1, z + 1] - ey)
        hy = (-courant) * (aelec[0, z + 1] - ex)
        hz = (-courant) * ((next_x1 - ey) - (next_y0 - ex))
        amagn[0, z + 1] = hx
        amagn[1, z + 1] = hy
        amagn[2, z + 1] = hz
        row_send[5, 0, pl.ds(z, 1)] = hy[nx - 1:nx]
        row_send[5, 1, pl.ds(z, 1)] = hz[nx - 1:nx]
        return pack_last(hz, nz + z, pack_last(hx, z, packed))

    col_send[5] = each_z(adjoint_magnetic, blank)
    send_halo(5)

    loads["far_y"].wait()

    def project(tick):
        total = 0.0
        for slot in range(gy):
            total = total + triple(split(planes[tick, slot]), (far_y[tick, slot, 0], far_y[tick, slot, 1]))
        return total

    arrive(first_planes)
    early = project(0)
    arrive(second_planes)
    half = early + project(1)
    for c in range(2):
        qall[c, mx] = half[c * nx:(c + 1) * nx]
    start(q_copies)

    take_halo(5)

    def adjoint_second(z, carry):
        gain = courant * inv[z]
        curl_x, curl_y, curl_z = curls(amagn, 5, z)
        lit = src[...] == z
        afinal[0, z] = aelec[0, z] + gain * (curl_x - jnp.where(lit, drive[0:nx, ny:2 * ny], 0.0))
        afinal[1, z] = aelec[1, z] + gain * (curl_y - jnp.where(lit, drive[nx:2 * nx, ny:2 * ny], 0.0))
        afinal[2, z] = gain * curl_z
        return carry

    each_z(adjoint_second, 0)
    stores.append(pltpu.make_async_copy(afinal, adj_out, out_sems.at[1]))
    stores[1].start()

    loads["far_x"].wait()
    arrive(q_copies)
    for c in range(2):
        high, low = split(jnp.reshape(qall[c], (gx * nx, freqs * 2 * nb)))
        for f in range(freqs):
            cut = slice(f * 2 * nb, (f + 1) * 2 * nb)
            both = triple((far_x[f, 0], far_x[f, 1]), (high[:, cut], low[:, cut]))
            far[f, c, 0] = both[0:na, 0:nb] + both[na:2 * na, nb:2 * nb]
            far[f, c, 1] = both[0:na, nb:2 * nb] - both[na:2 * na, 0:nb]
    stores.append(pltpu.make_async_copy(far, far_out, out_sems.at[2]))
    stores[2].start()

    for number in range(6):
        end_halo(number)
    for copies in (v_copies, g_copies, first_planes, second_planes, q_copies):
        left(copies)
    for copy in stores:
        copy.wait()


def per_device(consts, gx, gy, e_field, h_field, inverse_permittivity, monitor_layer, source_layer, residual_far):
    _, nz, nx, ny = e_field.shape
    freqs = len(factors)
    na, nb = residual_far.shape[3:]
    f32 = jnp.float32
    shapes = [
        pltpu.VMEM((3, nz + 1, nx, ny), f32),
        pltpu.VMEM((3, nz + 1, nx, ny), f32),
        pltpu.VMEM(inverse_permittivity.shape, f32),
        pltpu.VMEM(monitor_layer.shape, jnp.int32),
        pltpu.VMEM(source_layer.shape, jnp.int32),
        pltpu.VMEM(residual_far.shape, f32),
    ] + [pltpu.VMEM(const.shape[1:], jnp.bfloat16) for const in consts] + [
        pltpu.VMEM((2, nz + 1, nx, ny), f32),
        pltpu.VMEM((3, nz + 1, nx, ny), f32),
        pltpu.VMEM((3, nz, nx, ny), f32),
        pltpu.VMEM(residual_far.shape, f32),
        pltpu.VMEM((6, 2, nz, ny), f32),
        pltpu.VMEM((6, nx, ny), f32),
        pltpu.VMEM((6, 2, nz, ny), f32),
        pltpu.VMEM((6, nx, ny), f32),
        pltpu.VMEM((gx, freqs, 2 * nx, 2 * nb), f32),
        pltpu.VMEM((gx, freqs, 2 * nx, 2 * nb), f32),
        pltpu.VMEM((gy, freqs, 2 * nx, 2 * nb), f32),
        pltpu.VMEM((len(ticks), gy, 2 * nx, ny), f32),
        pltpu.VMEM((2, gx, nx, freqs * 2 * nb), f32),
    ]
    dma = pltpu.SemaphoreType.DMA
    shapes += [dma((10,)), dma((3,)), dma((6, 2)), dma((6, 2)), dma((gx,)), dma((gx,)), dma((gy,)), dma((gy,)),
               dma((len(ticks), gy)), dma((len(ticks), gy)), dma((gx,)), dma((gx,))]
    anywhere = pl.BlockSpec(memory_space=pl.ANY)
    return pl.pallas_call(
        functools.partial(kernel, gx, gy),
        out_shape=(
            jax.ShapeDtypeStruct(e_field.shape, f32),
            jax.ShapeDtypeStruct(residual_far.shape, f32),
            jax.ShapeDtypeStruct(e_field.shape, f32),
        ),
        in_specs=[anywhere] * 10,
        out_specs=(anywhere,) * 3,
        scratch_shapes=shapes,
        compiler_params=pltpu.CompilerParams(
            collective_id=0, has_side_effects=True, vmem_limit_bytes=40 * 1024 * 1024
        ),
    )(e_field, h_field, inverse_permittivity, monitor_layer, source_layer, residual_far, *consts)


def solution(mesh):
    in_specs = (
        P("design", None, "gx", "gy"),
        P("design", None, "gx", "gy"),
        P("design", "gx", "gy"),
        P(("design", "gx"), "gy"),
        P(("design", "gx"), "gy"),
        P("design", None, None, "gx", "gy"),
    )
    out_specs = (
        P("design", None, "gx", "gy"),
        P("design", None, None, "gx", "gy"),
        P("design", None, "gx", "gy"),
    )
    gx, gy = mesh.shape["gx"], mesh.shape["gy"]

    def local(e_field, h_field, inverse_permittivity, monitor_layer, source_layer, residual_far):
        _, _, nx, ny = e_field.shape
        na, nb = residual_far.shape[3:]
        consts = [jnp.asarray(table) for table in tables(gx, gy, na, nb, nx, ny)]
        return per_device(consts, gx, gy, e_field, h_field, inverse_permittivity, monitor_layer,
                          source_layer, residual_far)

    return jax.shard_map(local, mesh=mesh, in_specs=in_specs, out_specs=out_specs, check_vma=False)
```

time: 231 us -> 40.8 us (0.18)
  local copies, waits for them, and re-layouts: 71.8 us -> 13.9 us
  waiting for transfers between devices: 50.7 us -> 0 us
  starting transfers between devices: 39.6 us -> 0 us
  blocking collectives: 25.8 us -> 0 us
  Pallas kernels: 0 us -> 25.7 us
  other arithmetic: 17.8 us -> 0 us
  between operations: 15.1 us -> 0.66 us
  matrix products: 8.31 us -> 0 us
    unnamed x5 -> x0, waiting for transfers between devices: 39.9 us -> none
    ppermute x16 -> x0, starting transfers between devices: 39.5 us -> none  [from_behind(): lax.ppermute(value, axis, [(source, source + steps) for source in range(l...]
    all_gather x1 -> x0, blocking collectives: 25.8 us -> none  [per_device(): piece = lax.all_gather(residual_far, 'gy', axis=4, tiled=True)]
    pallas_call x0 -> x1, Pallas kernels: none -> 25.7 us  [per_device(): pl.pallas_call(functools.partial(kernel, gx, gy), out_shape=(jax.ShapeDty...]
    slice x48 -> x0, local copies, waits for them, and re-layouts: 18.6 us -> none  [the longest x4 1.82 us: step_electric(): magn[2][:, -1:, :]]
    unnamed x142 -> x23, local copies, waits for them, and re-layouts: 30 us -> 13.9 us
    ppermute x16 -> x0, waiting for transfers between devices: 10.8 us -> none  [from_behind(): lax.ppermute(value, axis, [(source, source + steps) for source in range(l...]
    squeeze x19 -> x0, local copies, waits for them, and re-layouts: 9.12 us -> none  [the longest x4 4.06 us: step_magnetic(): next_x2 = jnp.concatenate([elec[2][:, 1:, :], face_x[1]], axis=1)]
  transfers between devices with their start and end apart: 19 -> 0, of which waited for: 5 -> 0; matrix products, arithmetic and copies ran while one was open for 26% -> 0% of each run, Pallas kernels for 0% -> 0%
where the time goes in v1:
time: 40.8 us; the launch traced here: 40.3 us
  Pallas kernels  25.7 us (63%)
  local copies, waits for them, and re-layouts  13.9 us (34%)
  between operations  0.66 us (2%)
    pallas_call x1, Pallas kernels, per_device(): pl.pallas_call(functools.partial(kernel, gx, gy), out_shape=(jax.ShapeDty...  25.7 us
    unnamed x23, local copies, waits for them, and re-layouts  13.9 us

profile of v1, /device:TPU:0, one launch (start us, length us, event | category | flops | bytes accessed | tf_op | source)
XLA Modules:
  0.0 40.3 jit_solution(5521795209712989394)
XLA Ops:
  0.6 0.0 copy-start
  0.6 2.2 %copy-done = bf16[4,4,2,2,128,256]{5,4,3,2,1,0:T(8,128)(2,1)S(1)} copy-done((bf16[4,4,2,2,128,256]{5,4,3,2,1,0:T(8,128)(2,1)S(1)}, bf16[4,4,2,2,128,256]{5,4,3,2,1,0:T(8,128)(2,1)}, u32[]{:S(2)}) %copy-start) | copy-done | bytes 4194328
  2.8 0.0 copy-start.1
  2.8 2.2 %copy-done.1 = bf16[4,2,4,2,128,256]{5,4,3,2,1,0:T(8,128)(2,1)S(1)} copy-done((bf16[4,2,4,2,128,256]{5,4,3,2,1,0:T(8,128)(2,1)S(1)}, bf16[4,2,4,2,128,256]{5,4,3,2,1,0:T(8,128)(2,1)}, u32[]{:S(2)}) %copy-start.1) | copy-done | bytes 4194328
  5.0 0.0 copy-start.2
  5.0 1.0 %copy-done.2 = bf16[4,2,2,128,128]{4,3,2,1,0:T(8,128)(2,1)S(1)} copy-done((bf16[4,2,2,128,128]{4,3,2,1,0:T(8,128)(2,1)S(1)}, bf16[4,2,2,128,128]{4,3,2,1,0:T(8,128)(2,1)}, u32[]{:S(2)}) %copy-start.2) | copy-done | bytes 524312
  6.1 0.0 copy-start.3
  6.1 1.0 %copy-done.3 = bf16[4,2,2,128,64]{4,3,2,1,0:T(8,128)(2,1)S(1)} copy-done((bf16[4,2,2,128,64]{4,3,2,1,0:T(8,128)(2,1)S(1)}, bf16[4,2,2,128,64]{4,3,2,1,0:T(8,128)(2,1)}, u32[]{:S(2)}) %copy-start.3) | copy-done | bytes 262168
  7.1 0.0 copy-start.4
  7.1 1.0 %copy-done.4 = f32[3,16,16,128]{3,2,1,0:T(8,128)S(1)} copy-done((f32[3,16,16,128]{3,2,1,0:T(8,128)S(1)}, f32[3,16,16,128]{3,2,1,0:T(8,128)}, u32[]{:S(2)}) %copy-start.4) | copy-done | bytes 393240
  8.1 0.0 copy-start.5
  8.1 1.0 %copy-done.5 = f32[3,16,16,128]{3,2,1,0:T(8,128)S(1)} copy-done((f32[3,16,16,128]{3,2,1,0:T(8,128)S(1)}, f32[3,16,16,128]{3,2,1,0:T(8,128)}, u32[]{:S(2)}) %copy-start.5) | copy-done | bytes 393240
  9.1 0.0 copy-start.6
  9.1 0.9 %copy-done.6 = f32[2,2,2,64,64]{4,3,2,1,0:T(8,128)S(1)} copy-done((f32[2,2,2,64,64]{4,3,2,1,0:T(8,128)S(1)}, f32[2,2,2,64,64]{4,3,2,1,0:T(8,128)}, u32[]{:S(2)}) %copy-start.6) | copy-done | bytes 131096
  10.0 0.0 copy-start.7
  10.0 0.9 %copy-done.7 = f32[16,16,128]{2,1,0:T(8,128)S(1)} copy-done((f32[16,16,128]{2,1,0:T(8,128)S(1)}, f32[16,16,128]{2,1,0:T(8,128)}, u32[]{:S(2)}) %copy-start.7) | copy-done | bytes 131096
  10.9 0.0 copy-start.8
  10.9 0.7 %copy-done.8 = s32[16,128]{1,0:T(8,128)S(1)} copy-done((s32[16,128]{1,0:T(8,128)S(1)}, s32[16,128]{1,0:T(8,128)}, u32[]{:S(2)}) %copy-start.8) | copy-done | bytes 8216
  11.6 0.0 copy-start.9
  11.6 0.7 %copy-done.9 = s32[16,128]{1,0:T(8,128)S(1)} copy-done((s32[16,128]{1,0:T(8,128)S(1)}, s32[16,128]{1,0:T(8,128)}, u32[]{:S(2)}) %copy-start.9) | copy-done | bytes 8216
  12.3 25.7 %shard_map.121 = (f32[3,16,16,128]{3,2,1,0:T(8,128)S(1)}, f32[2,2,2,64,64]{4,3,2,1,0:T(8,128)S(1)}, f32[3,16,16,128]{3,2,1,0:T(8,128)S(1)}) custom-call(f32[3,16,16,128]{3,2,1,0:T(8,128)S(1)} %copy-done.4, f32[3,16,16,128]{3,2,1,0:T(8,128)S(1)} %copy-done.5, f32[16,16,128]{2,1,0:T(8,128)S(1)} %copy-done.7, s32[16,128]{1,0:T(8,128)S(1)} %copy-done.8, ...), custom_call_target="tpu_custom_call" | custom-call | tf_op jit(solution)/shard_map/pallas_call | solution.py:453
  38.1 0.7 %copy.16 = f32[3,16,16,128]{3,2,1,0:T(8,128)} copy(f32[3,16,16,128]{3,2,1,0:T(8,128)S(1)} %get-tuple-element.6) | data formatting | bytes 786432
  38.8 0.7 %copy.17 = f32[2,2,2,64,64]{4,3,2,1,0:T(8,128)} copy(f32[2,2,2,64,64]{4,3,2,1,0:T(8,128)S(1)} %get-tuple-element.7) | data formatting | bytes 262144
  39.5 0.7 %copy.18 = f32[3,16,16,128]{3,2,1,0:T(8,128)} copy(f32[3,16,16,128]{3,2,1,0:T(8,128)S(1)} %get-tuple-element.8) | data formatting | bytes 786432
Async XLA Ops:
  0.6 2.2 %copy-start = (bf16[4,4,2,2,128,256]{5,4,3,2,1,0:T(8,128)(2,1)S(1)}, bf16[4,4,2,2,128,256]{5,4,3,2,1,0:T(8,128)(2,1)}, u32[]{:S(2)}) copy-start(bf16[4,4,2,2,128,256]{5,4,3,2,1,0:T(8,128)(2,1)} %constant.9.clone.back_y_in) | copy-start | bytes 12582916
  2.8 2.2 %copy-start.1 = (bf16[4,2,4,2,128,256]{5,4,3,2,1,0:T(8,128)(2,1)S(1)}, bf16[4,2,4,2,128,256]{5,4,3,2,1,0:T(8,128)(2,1)}, u32[]{:S(2)}) copy-start(bf16[4,2,4,2,128,256]{5,4,3,2,1,0:T(8,128)(2,1)} %constant.8.clone.far_y_in) | copy-start | bytes 12582916
  5.0 1.0 %copy-start.2 = (bf16[4,2,2,128,128]{4,3,2,1,0:T(8,128)(2,1)S(1)}, bf16[4,2,2,128,128]{4,3,2,1,0:T(8,128)(2,1)}, u32[]{:S(2)}) copy-start(bf16[4,2,2,128,128]{4,3,2,1,0:T(8,128)(2,1)} %constant.11.clone.back_x_in) | copy-start | bytes 1572868
  6.1 1.0 %copy-start.3 = (bf16[4,2,2,128,64]{4,3,2,1,0:T(8,128)(2,1)S(1)}, bf16[4,2,2,128,64]{4,3,2,1,0:T(8,128)(2,1)}, u32[]{:S(2)}) copy-start(bf16[4,2,2,128,64]{4,3,2,1,0:T(8,128)(2,1)} %constant.10.clone.far_x_in) | copy-start | bytes 786436
  7.1 1.0 %copy-start.4 = (f32[3,16,16,128]{3,2,1,0:T(8,128)S(1)}, f32[3,16,16,128]{3,2,1,0:T(8,128)}, u32[]{:S(2)}) copy-start(f32[3,16,16,128]{3,2,1,0:T(8,128)} %e_in.1) | copy-start | bytes 1179652
  8.1 1.0 %copy-start.5 = (f32[3,16,16,128]{3,2,1,0:T(8,128)S(1)}, f32[3,16,16,128]{3,2,1,0:T(8,128)}, u32[]{:S(2)}) copy-start(f32[3,16,16,128]{3,2,1,0:T(8,128)} %h_in.1) | copy-start | bytes 1179652
  9.1 0.9 %copy-start.6 = (f32[2,2,2,64,64]{4,3,2,1,0:T(8,128)S(1)}, f32[2,2,2,64,64]{4,3,2,1,0:T(8,128)}, u32[]{:S(2)}) copy-start(f32[2,2,2,64,64]{4,3,2,1,0:T(8,128)} %res_in.1) | copy-start | bytes 393220
  10.0 0.9 %copy-start.7 = (f32[16,16,128]{2,1,0:T(8,128)S(1)}, f32[16,16,128]{2,1,0:T(8,128)}, u32[]{:S(2)}) copy-start(f32[16,16,128]{2,1,0:T(8,128)} %k_in.1) | copy-start | bytes 393220
  10.9 0.7 %copy-start.8 = (s32[16,128]{1,0:T(8,128)S(1)}, s32[16,128]{1,0:T(8,128)}, u32[]{:S(2)}) copy-start(s32[16,128]{1,0:T(8,128)} %mon_in.1) | copy-start | bytes 24580
  11.6 0.7 %copy-start.9 = (s32[16,128]{1,0:T(8,128)S(1)}, s32[16,128]{1,0:T(8,128)}, u32[]{:S(2)}) copy-start(s32[16,128]{1,0:T(8,128)} %src_in.1) | copy-start | bytes 24580
